TPU v7x, 32 devices: a whole 2x2x4 slice. The times are simulated.
32 devices in a mesh: groups: 2 (over y), dp: 4 (over z), mp: 2 (over x), sub: 2 (over core).
Axes of the slice: x: 2, y: 2, z: 4, core: 2. Of those that a mesh axis runs over, the one named last changes fastest.
Arguments:
- hidden: bfloat16 [4096, 14336], P(('groups', 'dp', 'sub'), 'mp'), parts along dimension 0, may hold values from -6 to 6
- out_grad: bfloat16 [4096, 4096], P(('groups', 'dp', 'sub'), 'mp'), parts along dimension 0, may hold values from -80 to 80
- lengths: int32 [64], P(('groups', 'dp', 'sub')), parts along dimension 0, may hold values from 16 to 64
- proj_in: bfloat16 [14336, 32], P('mp'), may hold values from -0.005859375 to 0.005859375
- proj_out: bfloat16 [4096, 32], P('mp'), may hold values from -0.09375 to 0.09375
- test_proj: bfloat16 [2048, 1024], P(('mp', 'sub')), may hold values from -6 to 6
Outputs:
- covariance: float32 [2048, 1024], P(('groups', 'dp', 'sub')), parts along dimension 0
- scores: float32 [64, 2048], P(('groups', 'dp', 'sub'), 'mp'), parts along dimension 0
There are 2 independent parts, one for each index of `groups`. A program takes and returns all parts, laid end to end along the dimension named above; an argument that names none is the same for every part. Nothing has to cross between parts.
All inputs are finite; a program needn't handle non-finite values.
Results may differ from a plain program's by a relative error of at most 0.004.
Values may be sent and summed in bfloat16 or wider, within the bound.
No kernel may reach another device: no remote copies, remote signals or barrier semaphores. Data moves between devices by JAX's collectives and lax.ppermute only.
A program may use at most 64 MiB of HBM per device.

v0:
```python
import functools

import jax
import jax.numpy as jnp
from jax import lax
from jax.experimental import pallas as pl
from jax.experimental.pallas import tpu as pltpu
from jax.sharding import PartitionSpec as P

SEQ = 64
CHUNK = 1024
CONTRACT_LAST = (((1,), (1,)), ((), ()))
CONTRACT_FIRST = (((0,), (0,)), ((), ()))


def chunks_of(width):
    return [(at, min(CHUNK, width - at)) for at in range(0, width, CHUNK)]


def project_kernel(hidden, out_grad, proj_in, proj_out, out, hid, og, pin, pout, sems):
    jobs = []
    for src, src_w, dst, dst_w in ((out_grad, proj_out, og, pout), (hidden, proj_in, hid, pin)):
        for at, size in chunks_of(src.shape[1]):
            jobs.append((src.at[:, pl.ds(at, size)], dst.at[:, pl.ds(at, size)],
                         src_w.at[:, pl.ds(at, size)], dst_w.at[:, pl.ds(at, size)]))
    copies = []
    for n, (src, dst, src_w, dst_w) in enumerate(jobs):
        pair = (pltpu.make_async_copy(src_w, dst_w, sems.at[1, n]), pltpu.make_async_copy(src, dst, sems.at[0, n]))
        for copy in pair:
            copy.start()
        copies.append(pair)
    first = len(chunks_of(out_grad.shape[1]))
    sums = [None, None]
    for n, (_, dst, _, dst_w) in enumerate(jobs):
        for copy in copies[n]:
            copy.wait()
        part = lax.dot_general(dst_w[...], dst[...], CONTRACT_LAST, preferred_element_type=jnp.float32)
        which = 0 if n >= first else 1
        sums[which] = part if sums[which] is None else sums[which] + part
    k_in = pin.shape[0]
    out[:k_in] = sums[0]
    out[k_in:] = sums[1]


def project(hidden, out_grad, proj_in, proj_out):
    rows, width = hidden.shape
    narrow = out_grad.shape[1]
    k_in, k_out = proj_in.shape[1], proj_out.shape[1]
    jobs = len(chunks_of(width)) + len(chunks_of(narrow))
    return pl.pallas_call(
        project_kernel,
        out_shape=jax.ShapeDtypeStruct((k_in + k_out, rows), jnp.float32),
        in_specs=[pl.BlockSpec(memory_space=pltpu.HBM)] * 4,
        out_specs=pl.BlockSpec(memory_space=pltpu.VMEM),
        scratch_shapes=[
            pltpu.VMEM((rows, width), jnp.bfloat16),
            pltpu.VMEM((rows, narrow), jnp.bfloat16),
            pltpu.VMEM((k_in, width), jnp.bfloat16),
            pltpu.VMEM((k_out, narrow), jnp.bfloat16),
            pltpu.SemaphoreType.DMA((2, jobs)),
        ],
        compiler_params=pltpu.CompilerParams(vmem_limit_bytes=24 << 20),
        cost_estimate=pl.CostEstimate(
            flops=2 * rows * (width * k_in + narrow * k_out),
            bytes_accessed=2 * rows * (width + narrow) + 2 * (width * k_in + narrow * k_out),
            transcendentals=0,
        ),
    )(*(pltpu.with_memory_space_constraint(x, pltpu.HBM) for x in (hidden, out_grad, proj_in.T, proj_out.T)))


def grads_kernel(k_in, mask, *refs):
    *pieces, out = refs
    both = pieces[0][...]
    for piece in pieces[1:]:
        both = both + piece[...]
    rows = both.shape[1]
    act = both[:k_in] * mask[...]
    grad = both[k_in:]
    row = lax.broadcasted_iota(jnp.int32, (16, rows), 0)
    col = lax.broadcasted_iota(jnp.int32, (16, rows), 1)
    pick = jnp.where((col >= row * SEQ) & (col < (row + 1) * SEQ), 1.0, 0.0).astype(jnp.bfloat16)
    per = 8
    k_out = grad.shape[0]
    for at in range(0, k_in, per):
        rest = jnp.concatenate([act[i:i + 1] * grad for i in range(at, at + per)], axis=0)
        total = None
        for _ in range(3):
            high = rest.astype(jnp.bfloat16)
            rest = rest - high.astype(jnp.float32)
            part = lax.dot_general(pick, high, CONTRACT_LAST, preferred_element_type=jnp.float32)
            total = part if total is None else total + part
        out[:, at * k_out:(at + per) * k_out] = total[:out.shape[0]].astype(jnp.bfloat16)


def example_grads(mask, pieces, k_in, k_out):
    vmem = pl.BlockSpec(memory_space=pltpu.VMEM)
    return pl.pallas_call(
        functools.partial(grads_kernel, k_in),
        out_shape=jax.ShapeDtypeStruct((mask.shape[1] // SEQ, k_in * k_out), jnp.bfloat16),
        in_specs=[vmem] * (1 + len(pieces)),
        out_specs=vmem,
        compiler_params=pltpu.CompilerParams(vmem_limit_bytes=6 << 20),
        cost_estimate=pl.CostEstimate(flops=1 << 33, bytes_accessed=0, transcendentals=0),
    )(mask, *pieces)


def finish_kernel(examples, n_pieces, n_raw, *refs):
    pieces, raw = refs[:n_pieces], refs[n_pieces:n_pieces + n_raw]
    cov, scores = refs[n_pieces + n_raw:]
    own_rows = cov.shape[0]
    place = lax.axis_index(("dp", "sub"))
    every = jnp.concatenate([p[...] for p in pieces], axis=0)
    if own_rows % 128 == 0:
        at = pl.multiple_of(place * own_rows, own_rows)
        own = jnp.concatenate([p[:, pl.ds(at, own_rows)] for p in pieces], axis=0)
    else:
        at = pl.multiple_of((place * own_rows) // 128 * 128, 128)
        wider = jnp.concatenate([p[:, pl.ds(at, 128)] for p in pieces], axis=0)
        own = pltpu.roll(wider.astype(jnp.float32), at - place * own_rows + 128, 1)[:, :own_rows].astype(jnp.bfloat16)
    wide = every.astype(jnp.float32)
    factor = lax.rsqrt(jnp.sum(wide * wide) / examples + 1e-06)
    if n_raw == 2:
        near, far = raw[0][...], raw[1][...]
        first = lax.axis_index("sub") == 0
        half = near.shape[1]
        scores[:, :half] = jnp.where(first, near, far) * factor
        scores[:, half:] = jnp.where(first, far, near) * factor
    else:
        scores[...] = raw[0][...] * factor
    cov[...] = lax.dot_general(own, every, CONTRACT_FIRST, preferred_element_type=jnp.float32) * (1.0 / examples)


def finish(examples, own_rows, pieces, raw):
    flat = pieces[0].shape[1]
    vmem = pl.BlockSpec(memory_space=pltpu.VMEM)
    return pl.pallas_call(
        functools.partial(finish_kernel, examples, len(pieces), len(raw)),
        out_shape=(
            jax.ShapeDtypeStruct((own_rows, flat), jnp.float32),
            jax.ShapeDtypeStruct((raw[0].shape[0], sum(r.shape[1] for r in raw)), jnp.float32),
        ),
        in_specs=[vmem] * (len(pieces) + len(raw)),
        out_specs=(vmem, vmem),
        compiler_params=pltpu.CompilerParams(vmem_limit_bytes=8 << 20),
    )(*pieces, *raw)


def per_device(hidden, out_grad, lengths, proj_in, proj_out, test_proj):
    k_in, k_out = proj_in.shape[1], proj_out.shape[1]
    flat = k_in * k_out
    rows = hidden.shape[0]
    group = ("dp", "sub")
    sharers = lax.axis_size(group)
    examples = lengths.shape[0] * sharers
    n_sub = lax.axis_size("sub")

    both = project(hidden, out_grad, proj_in, proj_out)
    if lax.axis_size("mp") == 2:
        pieces = [both, lax.ppermute(both, "mp", [(0, 1), (1, 0)])]
    else:
        pieces = [lax.psum(both, "mp")]
    lengths, _ = lax.optimization_barrier((lengths, both))
    slots = jnp.arange(SEQ, dtype=jnp.int32)
    mask = (slots[None, :] < lengths[:, None]).astype(jnp.float32).reshape(1, rows)
    grads = example_grads(mask, pieces, k_in, k_out)

    if n_sub == 2:
        other = lax.ppermute(test_proj, "sub", [(0, 1), (1, 0)])
        tests = [test_proj, other]
    else:
        tests = [lax.all_gather(test_proj, "sub", axis=0, tiled=True)]
    raw = [jnp.einsum("ep,qp->eq", grads, t, preferred_element_type=jnp.float32) for t in tests]

    if sharers in (2, 4, 8):
        held = grads
        step = sharers // 2
        while True:
            came = lax.ppermute(held, group, [(i, i ^ step) for i in range(sharers)])
            if step == 1:
                break
            held = jnp.concatenate([held, came], axis=0)
            step //= 2
        gathered = [held, came]
    else:
        gathered = [lax.all_gather(grads, group, axis=0, tiled=True)]
    return finish(examples, flat // sharers, gathered, raw)


def solution(mesh):
    in_specs = (
        P(("groups", "dp", "sub"), "mp"),
        P(("groups", "dp", "sub"), "mp"),
        P(("groups", "dp", "sub")),
        P("mp", None),
        P("mp", None),
        P(("mp", "sub"), None),
    )
    out_specs = (P(("groups", "dp", "sub"), None), P(("groups", "dp", "sub"), "mp"))
    return jax.shard_map(
        per_device, mesh=mesh, in_specs=in_specs, out_specs=out_specs, check_vma=False
    )
```

profile of v0, /device:TPU:0, one launch (start us, length us, event | category | flops | bytes accessed | tf_op | source)
XLA Modules:
  0.0 21.6 jit_solution(4647118982217890226)
XLA Ops:
  0.6 0.0 copy-start
  0.6 0.0 copy-start.1
  0.7 4.2 %shard_map.77.refs_0_ = f32[64,256]{1,0:T(8,128)S(1)} custom-call(bf16[256,7168]{1,0:T(8,128)(2,1)} %hidden.1, bf16[256,2048]{1,0:T(8,128)(2,1)} %out_grad.1, bf16[32,7168]{1,0:T(8,128)(2,1)} %bitcast.6, bf16[32,2048]{1,0:T(8,128)(2,1)} %bitcast.7), custom_call_target="tpu_custom_call" | custom-call | flops 150994944 | bytes 5308416 | tf_op jit(solution)/shard_map/pallas_call | solution.py:50
  4.9 3.0 %collective-permute-start = (f32[64,256]{1,0:T(8,128)S(1)}, f32[64,256]{1,0:T(8,128)S(1)}, u32[]{:S(2)}, u32[]{:S(2)}) collective-permute-start(f32[64,256]{1,0:T(8,128)S(1)} %shard_map.77.refs_0_), channel_id=1, source_target_pairs={{0,2},{2,0},{1,3},{3,1},{4,6},{6,4},{5,7},{7,5},{8,10},{10,8},{9,1... | collective-permute-start | bytes 196616 | tf_op jit(solution)/shard_map/ppermute | solution.py:159
  7.9 0.0 copy-done
  7.9 0.0 collective-permute-start.4
  7.9 0.0 copy-done.1
  7.9 0.1 fusion
  8.0 0.1 reshape.33.mask
  8.1 2.1 %collective-permute-done.refs_1_ = f32[64,256]{1,0:T(8,128)S(1)} collective-permute-done((f32[64,256]{1,0:T(8,128)S(1)}, f32[64,256]{1,0:T(8,128)S(1)}, u32[]{:S(2)}, u32[]{:S(2)}) %collective-permute-start) | collective-permute-done | bytes 65568 | tf_op jit(solution)/shard_map/ppermute | solution.py:159
  10.1 0.5 %shard_map.78 = bf16[4,1024]{1,0:T(4,128)(2,1)S(1)} custom-call(f32[1,256]{1,0:T(1,128)S(1)} %reshape.33.mask, f32[64,256]{1,0:T(8,128)S(1)} %shard_map.77.refs_0_, f32[64,256]{1,0:T(8,128)S(1)} %collective-permute-done.refs_1_), custom_call_target="tpu_custom_call" | custom-call | flops 8589934592 | tf_op jit(solution)/shard_map/pallas_call | solution.py:97
  10.7 3.1 %collective-permute-start.1 = (bf16[4,1024]{1,0:T(4,128)(2,1)S(1)}, bf16[4,1024]{1,0:T(4,128)(2,1)S(1)}, u32[]{:S(2)}, u32[]{:S(2)}) collective-permute-start(bf16[4,1024]{1,0:T(4,128)(2,1)S(1)} %shard_map.78), channel_id=1, source_target_pairs={{0,8},{1,9},{4,12},{5,13},{8,0},{9,1},{12,4},{13,5},{2,10},{3,11},... | collective-permute-start | bytes 24584 | tf_op jit(solution)/shard_map/ppermute | solution.py:178
  13.8 1.6 %collective-permute-done.1 = bf16[4,1024]{1,0:T(4,128)(2,1)S(1)} collective-permute-done((bf16[4,1024]{1,0:T(4,128)(2,1)S(1)}, bf16[4,1024]{1,0:T(4,128)(2,1)S(1)}, u32[]{:S(2)}, u32[]{:S(2)}) %collective-permute-start.1) | collective-permute-done | bytes 8224 | tf_op jit(solution)/shard_map/ppermute | solution.py:178
  15.5 2.0 %collective-permute-start.2 = (bf16[8,1024]{1,0:T(8,128)(2,1)S(1)}, bf16[8,1024]{1,0:T(8,128)(2,1)S(1)}, u32[]{:S(2)}, u32[]{:S(2)}) collective-permute-start(bf16[8,1024]{1,0:T(8,128)(2,1)S(1)} %pad_maximum_fusion.1), channel_id=1, source_target_pairs={{0,4},{1,5},{4,0},{5,1},{8,12},{9,13},{12,8},{13,9},{2,6},{3,7},{6... | collective-permute-start | bytes 49160 | tf_op jit(solution)/shard_map/ppermute | solution.py:178
  17.4 0.4 %fusion.1.refs_2_ = f32[4,512]{1,0:T(4,128)S(1)} fusion(bf16[4,1024]{1,0:T(4,128)(2,1)S(1)} %shard_map.78, bf16[512,1024]{1,0:T(8,128)(2,1)S(1)} %copy-done), kind=kOutput, calls=%fused_computation.4 | convolution fusion | flops 4194304 | bytes 1064960 | tf_op jit(solution)/shard_map/ep,qp->eq/dot_general | solution.py:172
  17.8 1.5 %collective-permute-done.2 = bf16[8,1024]{1,0:T(8,128)(2,1)S(1)} collective-permute-done((bf16[8,1024]{1,0:T(8,128)(2,1)S(1)}, bf16[8,1024]{1,0:T(8,128)(2,1)S(1)}, u32[]{:S(2)}, u32[]{:S(2)}) %collective-permute-start.2) | collective-permute-done | bytes 16416 | tf_op jit(solution)/shard_map/ppermute | solution.py:178
  19.3 0.1 collective-permute-start.3
  19.4 0.0 collective-permute-done.4
  19.4 0.4 %fusion.2.refs_3_ = f32[4,512]{1,0:T(4,128)S(1)} fusion(bf16[4,1024]{1,0:T(4,128)(2,1)S(1)} %shard_map.78, bf16[512,1024]{1,0:T(8,128)(2,1)S(1)} %collective-permute-done.4), kind=kOutput, calls=%fused_computation.5 | convolution fusion | flops 4194304 | bytes 1064960 | tf_op jit(solution)/shard_map/ep,qp->eq/dot_general | solution.py:172
  19.8 0.8 %collective-permute-done.3.refs_1_ = bf16[16,1024]{1,0:T(8,128)(2,1)S(1)} collective-permute-done((bf16[16,1024]{1,0:T(8,128)(2,1)S(1)}, bf16[16,1024]{1,0:T(8,128)(2,1)S(1)}, u32[]{:S(2)}, u32[]{:S(2)}) %collective-permute-start.3) | collective-permute-done | bytes 32800 | tf_op jit(solution)/shard_map/ppermute | solution.py:178
  20.6 1.1 %shard_map.79 = (f32[128,1024]{1,0:T(8,128)}, f32[4,1024]{1,0:T(4,128)}) custom-call(bf16[16,1024]{1,0:T(8,128)(2,1)S(1)} %pad_maximum_fusion.refs_0_, bf16[16,1024]{1,0:T(8,128)(2,1)S(1)} %collective-permute-done.3.refs_1_, f32[4,512]{1,0:T(4,128)S(1)} %fusion.1.refs_2_, f32[4,512]{1,0:T(4,128)S(1)} %fusion.2.refs_3_), custom_call_target="tpu_custom_call" | custom-call | tf_op jit(solution)/shard_map/pallas_call | solution.py:136
  (2 shorter events, 0.0 us)
Async XLA Ops:
  0.6 7.3 %copy-start = (bf16[512,1024]{1,0:T(8,128)(2,1)S(1)}, bf16[512,1024]{1,0:T(8,128)(2,1)}, u32[]{:S(2)}) copy-start(bf16[512,1024]{1,0:T(8,128)(2,1)} %param.11) | copy-start | bytes 3145732
  0.6 7.3 %copy-start.1 = (s32[4]{0:T(128)S(1)}, s32[4]{0:T(128)}, u32[]{:S(2)}) copy-start(s32[4]{0:T(128)} %param.8) | copy-start | bytes 52
  4.9 5.2 %collective-permute-start = (f32[64,256]{1,0:T(8,128)S(1)}, f32[64,256]{1,0:T(8,128)S(1)}, u32[]{:S(2)}, u32[]{:S(2)}) collective-permute-start(f32[64,256]{1,0:T(8,128)S(1)} %shard_map.77.refs_0_), channel_id=1, source_target_pairs={{0,2},{2,0},{1,3},{3,1},{4,6},{6,4},{5,7},{7,5},{8,10},{10,8},{9,1... | collective-permute-start | bytes 196616 | tf_op jit(solution)/shard_map/ppermute | solution.py:159
  7.9 11.5 %collective-permute-start.4 = (bf16[512,1024]{1,0:T(8,128)(2,1)S(1)}, bf16[512,1024]{1,0:T(8,128)(2,1)S(1)}, u32[]{:S(2)}, u32[]{:S(2)}) collective-permute-start(bf16[512,1024]{1,0:T(8,128)(2,1)S(1)} %copy-done), channel_id=1, source_target_pairs={{0,1},{1,0},{2,3},{3,2},{4,5},{5,4},{6,7},{7,6},{8,9},{9,8},{10,11... | collective-permute-start | bytes 3145736 | tf_op jit(solution)/shard_map/ppermute | solution.py:168
  10.7 4.8 %collective-permute-start.1 = (bf16[4,1024]{1,0:T(4,128)(2,1)S(1)}, bf16[4,1024]{1,0:T(4,128)(2,1)S(1)}, u32[]{:S(2)}, u32[]{:S(2)}) collective-permute-start(bf16[4,1024]{1,0:T(4,128)(2,1)S(1)} %shard_map.78), channel_id=1, source_target_pairs={{0,8},{1,9},{4,12},{5,13},{8,0},{9,1},{12,4},{13,5},{2,10},{3,11},... | collective-permute-start | bytes 24584 | tf_op jit(solution)/shard_map/ppermute | solution.py:178
  15.5 3.8 %collective-permute-start.2 = (bf16[8,1024]{1,0:T(8,128)(2,1)S(1)}, bf16[8,1024]{1,0:T(8,128)(2,1)S(1)}, u32[]{:S(2)}, u32[]{:S(2)}) collective-permute-start(bf16[8,1024]{1,0:T(8,128)(2,1)S(1)} %pad_maximum_fusion.1), channel_id=1, source_target_pairs={{0,4},{1,5},{4,0},{5,1},{8,12},{9,13},{12,8},{13,9},{2,6},{3,7},{6... | collective-permute-start | bytes 49160 | tf_op jit(solution)/shard_map/ppermute | solution.py:178
  19.3 1.3 %collective-permute-start.3 = (bf16[16,1024]{1,0:T(8,128)(2,1)S(1)}, bf16[16,1024]{1,0:T(8,128)(2,1)S(1)}, u32[]{:S(2)}, u32[]{:S(2)}) collective-permute-start(bf16[16,1024]{1,0:T(8,128)(2,1)S(1)} %pad_maximum_fusion.refs_0_), channel_id=1, source_target_pairs={{0,1},{1,0},{4,5},{5,4},{8,9},{9,8},{12,13},{13,12},{2,3},{3,2},{6... | collective-permute-start | bytes 98312 | tf_op jit(solution)/shard_map/ppermute | solution.py:178
where the time goes:
time: 21.8 us; the launch traced here: 21.6 us
  starting transfers between devices  8.19 us (38%)
  waiting for transfers between devices  5.98 us (27%)
  Pallas kernels  5.84 us (27%)
  matrix products  0.74 us (3%)
  between operations  0.69 us (3%)
    ppermute x3, starting transfers between devices, per_device(): came = lax.ppermute(held, group, [(i, i ^ step) for i in range(sharers)])  5.18 us
    pallas_call x1, Pallas kernels, project(): pl.pallas_call(project_kernel, out_shape=jax.ShapeDtypeStruct((k_in + k_o...  4.23 us
    ppermute x3, waiting for transfers between devices, per_device(): came = lax.ppermute(held, group, [(i, i ^ step) for i in range(sharers)])  3.9 us
    ppermute x1, starting transfers between devices, per_device(): pieces = [both, lax.ppermute(both, 'mp', [(0, 1), (1, 0)])]  3 us
    ppermute x1, waiting for transfers between devices, per_device(): pieces = [both, lax.ppermute(both, 'mp', [(0, 1), (1, 0)])]  2.08 us
    pallas_call x1, Pallas kernels, finish(): pl.pallas_call(functools.partial(finish_kernel, examples, len(pieces), le...  1.06 us
    dot_general x2, matrix products, per_device(): jnp.einsum('ep,qp->eq', grads, t, preferred_element_type=jnp.float32)  0.74 us
    pallas_call x1, Pallas kernels, example_grads(): pl.pallas_call(functools.partial(grads_kernel, k_in), out_shape=jax.Shape...  0.54 us
  transfers between devices with their start and end apart: 5, of which 4 were waited for; matrix products, arithmetic and copies ran while one was open for 4% of the time, Pallas kernels for 3%

commit v1 on v0

--- a/solution.py
+++ b/solution.py
@@ -8,45 +8,38 @@
 from jax.sharding import PartitionSpec as P
 
 SEQ = 64
-CHUNK = 1024
+ROWS = 64
 CONTRACT_LAST = (((1,), (1,)), ((), ()))
 CONTRACT_FIRST = (((0,), (0,)), ((), ()))
 
 
-def chunks_of(width):
-    return [(at, min(CHUNK, width - at)) for at in range(0, width, CHUNK)]
-
-
 def project_kernel(hidden, out_grad, proj_in, proj_out, out, hid, og, pin, pout, sems):
-    jobs = []
-    for src, src_w, dst, dst_w in ((out_grad, proj_out, og, pout), (hidden, proj_in, hid, pin)):
-        for at, size in chunks_of(src.shape[1]):
-            jobs.append((src.at[:, pl.ds(at, size)], dst.at[:, pl.ds(at, size)],
-                         src_w.at[:, pl.ds(at, size)], dst_w.at[:, pl.ds(at, size)]))
-    copies = []
-    for n, (src, dst, src_w, dst_w) in enumerate(jobs):
-        pair = (pltpu.make_async_copy(src_w, dst_w, sems.at[1, n]), pltpu.make_async_copy(src, dst, sems.at[0, n]))
-        for copy in pair:
-            copy.start()
-        copies.append(pair)
-    first = len(chunks_of(out_grad.shape[1]))
-    sums = [None, None]
-    for n, (_, dst, _, dst_w) in enumerate(jobs):
-        for copy in copies[n]:
-            copy.wait()
-        part = lax.dot_general(dst_w[...], dst[...], CONTRACT_LAST, preferred_element_type=jnp.float32)
-        which = 0 if n >= first else 1
-        sums[which] = part if sums[which] is None else sums[which] + part
+    rows = hidden.shape[0]
     k_in = pin.shape[0]
-    out[:k_in] = sums[0]
-    out[k_in:] = sums[1]
+    parts = [pl.ds(at, ROWS) for at in range(0, rows, ROWS)]
+    copies = [
+        pltpu.make_async_copy(proj_out, pout, sems.at[0]),
+        pltpu.make_async_copy(out_grad, og, sems.at[1]),
+        pltpu.make_async_copy(proj_in, pin, sems.at[2]),
+    ]
+    copies += [pltpu.make_async_copy(hidden.at[part], hid.at[part], sems.at[3 + n]) for n, part in enumerate(parts)]
+    for copy in copies:
+        copy.start()
+    for copy in copies[:2]:
+        copy.wait()
+    out[k_in:] = lax.dot_general(pout[...], og[...], CONTRACT_LAST, preferred_element_type=jnp.float32)
+    copies[2].wait()
+    sums = []
+    for part, copy in zip(parts, copies[3:]):
+        copy.wait()
+        sums.append(lax.dot_general(pin[...], hid[part], CONTRACT_LAST, preferred_element_type=jnp.float32))
+    out[:k_in] = jnp.concatenate(sums, axis=1)
 
 
 def project(hidden, out_grad, proj_in, proj_out):
     rows, width = hidden.shape
     narrow = out_grad.shape[1]
     k_in, k_out = proj_in.shape[1], proj_out.shape[1]
-    jobs = len(chunks_of(width)) + len(chunks_of(narrow))
     return pl.pallas_call(
         project_kernel,
         out_shape=jax.ShapeDtypeStruct((k_in + k_out, rows), jnp.float32),
@@ -57,7 +50,7 @@
             pltpu.VMEM((rows, narrow), jnp.bfloat16),
             pltpu.VMEM((k_in, width), jnp.bfloat16),
             pltpu.VMEM((k_out, narrow), jnp.bfloat16),
-            pltpu.SemaphoreType.DMA((2, jobs)),
+            pltpu.SemaphoreType.DMA((3 + rows // ROWS,)),
         ],
         compiler_params=pltpu.CompilerParams(vmem_limit_bytes=24 << 20),
         cost_estimate=pl.CostEstimate(
@@ -164,24 +157,19 @@
     mask = (slots[None, :] < lengths[:, None]).astype(jnp.float32).reshape(1, rows)
     grads = example_grads(mask, pieces, k_in, k_out)
 
-    if n_sub == 2:
-        other = lax.ppermute(test_proj, "sub", [(0, 1), (1, 0)])
-        tests = [test_proj, other]
+    if n_sub == 2 and sharers == 8:
+        swap = [(i, i ^ 1) for i in range(sharers)]
+        came = lax.ppermute(grads, group, swap)
+        held = jnp.concatenate([grads, came], axis=0)
+        gathered = [held]
+        for step in (2, 4, 6):
+            gathered.append(lax.ppermute(held, group, [(i, i ^ step) for i in range(sharers)]))
+        near = jnp.einsum("ep,qp->eq", grads, test_proj, preferred_element_type=jnp.float32)
+        for_other = jnp.einsum("ep,qp->eq", came, test_proj, preferred_element_type=jnp.float32)
+        raw = [near, lax.ppermute(for_other, group, swap)]
     else:
-        tests = [lax.all_gather(test_proj, "sub", axis=0, tiled=True)]
-    raw = [jnp.einsum("ep,qp->eq", grads, t, preferred_element_type=jnp.float32) for t in tests]
-
-    if sharers in (2, 4, 8):
-        held = grads
-        step = sharers // 2
-        while True:
-            came = lax.ppermute(held, group, [(i, i ^ step) for i in range(sharers)])
-            if step == 1:
-                break
-            held = jnp.concatenate([held, came], axis=0)
-            step //= 2
-        gathered = [held, came]
-    else:
+        tests = lax.all_gather(test_proj, "sub", axis=0, tiled=True)
+        raw = [jnp.einsum("ep,qp->eq", grads, tests, preferred_element_type=jnp.float32)]
         gathered = [lax.all_gather(grads, group, axis=0, tiled=True)]
     return finish(examples, flat // sharers, gathered, raw)
 

time: 21.8 us -> 22.1 us (1.014)
  waiting for transfers between devices: 5.98 us -> 6.51 us
  starting transfers between devices: 8.19 us -> 7.85 us
    ppermute x4 -> x5, waiting for transfers between devices: 3.9 us -> 4.42 us  [the longest x3 2.43 us: per_device(): lax.ppermute(held, group, [(i, i ^ step) for i in range(sharers)])]
    ppermute x4 -> x5, starting transfers between devices: 5.19 us -> 4.84 us  [the longest x3 4.84 us: per_device(): lax.ppermute(held, group, [(i, i ^ step) for i in range(sharers)])]
  transfers between devices with their start and end apart: 5 -> 6, of which waited for: 4 -> 4; matrix products, arithmetic and copies ran while one was open for 4% -> 4% of each run, Pallas kernels for 3% -> 0%
where the time goes in v1:
time: 22.1 us; the launch traced here: 21.9 us
  starting transfers between devices  7.85 us (36%)
  waiting for transfers between devices  6.51 us (29%)
  Pallas kernels  5.96 us (27%)
  matrix products  0.76 us (3%)
  between operations  0.67 us (3%)
    ppermute x3, starting transfers between devices, per_device(): lax.ppermute(held, group, [(i, i ^ step) for i in range(sharers)])  4.84 us
    pallas_call x1, Pallas kernels, project(): pl.pallas_call(project_kernel, out_shape=jax.ShapeDtypeStruct((k_in + k_o...  4.36 us
    ppermute x1, starting transfers between devices, per_device(): pieces = [both, lax.ppermute(both, 'mp', [(0, 1), (1, 0)])]  3 us
    ppermute x3, waiting for transfers between devices, per_device(): lax.ppermute(held, group, [(i, i ^ step) for i in range(sharers)])  2.43 us
    ppermute x1, waiting for transfers between devices, per_device(): pieces = [both, lax.ppermute(both, 'mp', [(0, 1), (1, 0)])]  2.09 us
    ppermute x1, waiting for transfers between devices, per_device(): came = lax.ppermute(grads, group, swap)  1.19 us
    pallas_call x1, Pallas kernels, finish(): pl.pallas_call(functools.partial(finish_kernel, examples, len(pieces), le...  1.06 us
    ppermute x1, waiting for transfers between devices, per_device(): raw = [near, lax.ppermute(for_other, group, swap)]  0.8 us
  transfers between devices with their start and end apart: 6, of which 4 were waited for; matrix products, arithmetic and copies ran while one was open for 4% of the time, Pallas kernels for 0%

profile of v1, /device:TPU:0, one launch (start us, length us, event | category | flops | bytes accessed | tf_op | source)
XLA Modules:
  0.0 21.9 jit_solution(16551887831729085682)
XLA Ops:
  0.6 0.0 copy-start
  0.6 0.0 copy-start.1
  0.7 4.4 %shard_map.77.refs_0_ = f32[64,256]{1,0:T(8,128)S(1)} custom-call(bf16[256,7168]{1,0:T(8,128)(2,1)} %hidden.1, bf16[256,2048]{1,0:T(8,128)(2,1)} %out_grad.1, bf16[32,7168]{1,0:T(8,128)(2,1)} %bitcast.6, bf16[32,2048]{1,0:T(8,128)(2,1)} %bitcast.7), custom_call_target="tpu_custom_call" | custom-call | flops 150994944 | bytes 5308416 | tf_op jit(solution)/shard_map/pallas_call | solution.py:43
  5.0 3.0 %collective-permute-start = (f32[64,256]{1,0:T(8,128)S(1)}, f32[64,256]{1,0:T(8,128)S(1)}, u32[]{:S(2)}, u32[]{:S(2)}) collective-permute-start(f32[64,256]{1,0:T(8,128)S(1)} %shard_map.77.refs_0_), channel_id=1, source_target_pairs={{0,2},{2,0},{1,3},{3,1},{4,6},{6,4},{5,7},{7,5},{8,10},{10,8},{9,1... | collective-permute-start | bytes 196616 | tf_op jit(solution)/shard_map/ppermute | solution.py:152
  8.0 0.0 copy-done.1
  8.0 0.1 fusion
  8.1 0.1 reshape.33.mask
  8.2 2.1 %collective-permute-done.refs_1_ = f32[64,256]{1,0:T(8,128)S(1)} collective-permute-done((f32[64,256]{1,0:T(8,128)S(1)}, f32[64,256]{1,0:T(8,128)S(1)}, u32[]{:S(2)}, u32[]{:S(2)}) %collective-permute-start) | collective-permute-done | bytes 65568 | tf_op jit(solution)/shard_map/ppermute | solution.py:152
  10.3 0.5 %shard_map.78 = bf16[4,1024]{1,0:T(4,128)(2,1)S(1)} custom-call(f32[1,256]{1,0:T(1,128)S(1)} %reshape.33.mask, f32[64,256]{1,0:T(8,128)S(1)} %shard_map.77.refs_0_, f32[64,256]{1,0:T(8,128)S(1)} %collective-permute-done.refs_1_), custom_call_target="tpu_custom_call" | custom-call | flops 8589934592 | tf_op jit(solution)/shard_map/pallas_call | solution.py:90
  10.8 0.0 collective-permute-start.1
  10.8 1.2 %collective-permute-done.1 = bf16[4,1024]{1,0:T(4,128)(2,1)S(1)} collective-permute-done((bf16[4,1024]{1,0:T(4,128)(2,1)S(1)}, bf16[4,1024]{1,0:T(4,128)(2,1)S(1)}, u32[]{:S(2)}, u32[]{:S(2)}) %collective-permute-start.1) | collective-permute-done | bytes 8224 | tf_op jit(solution)/shard_map/ppermute | solution.py:162
  12.0 4.2 %collective-permute-start.4 = (bf16[8,1024]{1,0:T(8,128)(2,1)S(1)}, bf16[8,1024]{1,0:T(8,128)(2,1)S(1)}, u32[]{:S(2)}, u32[]{:S(2)}) collective-permute-start(bf16[8,1024]{1,0:T(8,128)(2,1)S(1)} %pad_maximum_fusion.refs_0_), channel_id=1, source_target_pairs={{0,12},{1,13},{4,8},{5,9},{8,4},{9,5},{12,0},{13,1},{2,14},{3,15},... | collective-permute-start | bytes 49160 | tf_op jit(solution)/shard_map/ppermute | solution.py:166
  16.2 0.0 collective-permute-start.3
  16.2 0.6 %collective-permute-start.2 = (bf16[8,1024]{1,0:T(8,128)(2,1)S(1)}, bf16[8,1024]{1,0:T(8,128)(2,1)S(1)}, u32[]{:S(2)}, u32[]{:S(2)}) collective-permute-start(bf16[8,1024]{1,0:T(8,128)(2,1)S(1)} %pad_maximum_fusion.refs_0_), channel_id=1, source_target_pairs={{0,4},{1,5},{4,0},{5,1},{8,12},{9,13},{12,8},{13,9},{2,6},{3,7},{6... | collective-permute-start | bytes 49160 | tf_op jit(solution)/shard_map/ppermute | solution.py:166
  16.9 0.0 copy-done
  16.9 0.4 %fusion.2 = f32[4,512]{1,0:T(4,128)S(1)} fusion(bf16[4,1024]{1,0:T(4,128)(2,1)S(1)} %collective-permute-done.1, bf16[512,1024]{1,0:T(8,128)(2,1)S(1)} %copy-done), kind=kOutput, calls=%fused_computation.4 | convolution fusion | flops 4194304 | bytes 1064960 | tf_op jit(solution)/shard_map/ep,qp->eq/dot_general | solution.py:168
  17.2 0.0 collective-permute-start.5
  17.2 0.4 %fusion.1.refs_4_ = f32[4,512]{1,0:T(4,128)S(1)} fusion(bf16[4,1024]{1,0:T(4,128)(2,1)S(1)} %shard_map.78, bf16[512,1024]{1,0:T(8,128)(2,1)S(1)} %copy-done), kind=kOutput, calls=%fused_computation.3 | convolution fusion | flops 4194304 | bytes 1064960 | tf_op jit(solution)/shard_map/ep,qp->eq/dot_general | solution.py:167
  17.6 0.8 %collective-permute-done.5.refs_5_ = f32[4,512]{1,0:T(4,128)S(1)} collective-permute-done((f32[4,512]{1,0:T(4,128)S(1)}, f32[4,512]{1,0:T(4,128)S(1)}, u32[]{:S(2)}, u32[]{:S(2)}) %collective-permute-start.5) | collective-permute-done | bytes 8224 | tf_op jit(solution)/shard_map/ppermute | solution.py:169
  18.4 0.0 collective-permute-done.4.refs_3_
  18.4 2.4 %collective-permute-done.3.refs_2_ = bf16[8,1024]{1,0:T(8,128)(2,1)S(1)} collective-permute-done((bf16[8,1024]{1,0:T(8,128)(2,1)S(1)}, bf16[8,1024]{1,0:T(8,128)(2,1)S(1)}, u32[]{:S(2)}, u32[]{:S(2)}) %collective-permute-start.3) | collective-permute-done | bytes 16416 | tf_op jit(solution)/shard_map/ppermute | solution.py:166
  20.9 0.0 collective-permute-done.2.refs_1_
  20.9 1.1 %shard_map.79 = (f32[128,1024]{1,0:T(8,128)}, f32[4,1024]{1,0:T(4,128)}) custom-call(bf16[8,1024]{1,0:T(8,128)(2,1)S(1)} %pad_maximum_fusion.refs_0_, bf16[8,1024]{1,0:T(8,128)(2,1)S(1)} %collective-permute-done.2.refs_1_, bf16[8,1024]{1,0:T(8,128)(2,1)S(1)} %collective-permute-done.3.refs_2_, bf16[8,1024]{1,0:T(8,128)(2,1)S(1)} %collective-permute-done.4.refs_3_, ...), custom_call_target="tpu_custom_call" | custom-call | tf_op jit(solution)/shard_map/pallas_call | solution.py:129
  (1 shorter events, 0.0 us)
Async XLA Ops:
  0.6 16.2 %copy-start = (bf16[512,1024]{1,0:T(8,128)(2,1)S(1)}, bf16[512,1024]{1,0:T(8,128)(2,1)}, u32[]{:S(2)}) copy-start(bf16[512,1024]{1,0:T(8,128)(2,1)} %param.11) | copy-start | bytes 3145732
  0.6 7.4 %copy-start.1 = (s32[4]{0:T(128)S(1)}, s32[4]{0:T(128)}, u32[]{:S(2)}) copy-start(s32[4]{0:T(128)} %param.8) | copy-start | bytes 52
  5.0 5.2 %collective-permute-start = (f32[64,256]{1,0:T(8,128)S(1)}, f32[64,256]{1,0:T(8,128)S(1)}, u32[]{:S(2)}, u32[]{:S(2)}) collective-permute-start(f32[64,256]{1,0:T(8,128)S(1)} %shard_map.77.refs_0_), channel_id=1, source_target_pairs={{0,2},{2,0},{1,3},{3,1},{4,6},{6,4},{5,7},{7,5},{8,10},{10,8},{9,1... | collective-permute-start | bytes 196616 | tf_op jit(solution)/shard_map/ppermute | solution.py:152
  10.8 1.2 %collective-permute-start.1 = (bf16[4,1024]{1,0:T(4,128)(2,1)S(1)}, bf16[4,1024]{1,0:T(4,128)(2,1)S(1)}, u32[]{:S(2)}, u32[]{:S(2)}) collective-permute-start(bf16[4,1024]{1,0:T(4,128)(2,1)S(1)} %shard_map.78), channel_id=1, source_target_pairs={{0,1},{1,0},{4,5},{5,4},{8,9},{9,8},{12,13},{13,12},{2,3},{3,2},{6... | collective-permute-start | bytes 24584 | tf_op jit(solution)/shard_map/ppermute | solution.py:162
  12.0 6.4 %collective-permute-start.4 = (bf16[8,1024]{1,0:T(8,128)(2,1)S(1)}, bf16[8,1024]{1,0:T(8,128)(2,1)S(1)}, u32[]{:S(2)}, u32[]{:S(2)}) collective-permute-start(bf16[8,1024]{1,0:T(8,128)(2,1)S(1)} %pad_maximum_fusion.refs_0_), channel_id=1, source_target_pairs={{0,12},{1,13},{4,8},{5,9},{8,4},{9,5},{12,0},{13,1},{2,14},{3,15},... | collective-permute-start | bytes 49160 | tf_op jit(solution)/shard_map/ppermute | solution.py:166
  16.2 4.6 %collective-permute-start.3 = (bf16[8,1024]{1,0:T(8,128)(2,1)S(1)}, bf16[8,1024]{1,0:T(8,128)(2,1)S(1)}, u32[]{:S(2)}, u32[]{:S(2)}) collective-permute-start(bf16[8,1024]{1,0:T(8,128)(2,1)S(1)} %pad_maximum_fusion.refs_0_), channel_id=1, source_target_pairs={{0,8},{1,9},{4,12},{5,13},{8,0},{9,1},{12,4},{13,5},{2,10},{3,11},... | collective-permute-start | bytes 49160 | tf_op jit(solution)/shard_map/ppermute | solution.py:166
  16.2 4.6 %collective-permute-start.2 = (bf16[8,1024]{1,0:T(8,128)(2,1)S(1)}, bf16[8,1024]{1,0:T(8,128)(2,1)S(1)}, u32[]{:S(2)}, u32[]{:S(2)}) collective-permute-start(bf16[8,1024]{1,0:T(8,128)(2,1)S(1)} %pad_maximum_fusion.refs_0_), channel_id=1, source_target_pairs={{0,4},{1,5},{4,0},{5,1},{8,12},{9,13},{12,8},{13,9},{2,6},{3,7},{6... | collective-permute-start | bytes 49160 | tf_op jit(solution)/shard_map/ppermute | solution.py:166
  17.2 1.2 %collective-permute-start.5 = (f32[4,512]{1,0:T(4,128)S(1)}, f32[4,512]{1,0:T(4,128)S(1)}, u32[]{:S(2)}, u32[]{:S(2)}) collective-permute-start(f32[4,512]{1,0:T(4,128)S(1)} %fusion.2), channel_id=1, source_target_pairs={{0,1},{1,0},{4,5},{5,4},{8,9},{9,8},{12,13},{13,12},{2,3},{3,2},{6... | collective-permute-start | bytes 24584 | tf_op jit(solution)/shard_map/ppermute | solution.py:169
